TPU v7x, 1024 devices: a whole 4x4x32 slice. The times are simulated.
1024 devices in a mesh: expert: 64 (over z_lo, y), dp: 16 (over x, z_hi, core).
Axes of the slice: x: 4, y: 4, z: 32 (z_hi: 2, z_lo: 16; z = z_hi * 16 + z_lo), core: 2. Of those that a mesh axis runs over, the one named last changes fastest.
Arguments:
- tokens_in: bfloat16 [8192, 7168], P('expert', 'dp'), may hold values from -1.5 to 1.5
- grad_out: bfloat16 [8192, 7168], P('expert', 'dp'), may hold values from -1.5 to 1.5
- routes: int32 [8192, 2], P('expert'), may hold values from 0 to 31, all different within a row; in each aligned block of 128 rows (0 to 127, 128 to 255, ...) at most 12 rows name the same one
- gate_probs: float32 [8192, 2], P('expert'), may hold values from 0.1 to 1
- saved_gate: bfloat16 [64, 768, 512], P('expert'), may hold values from -6 to 6
- saved_up: bfloat16 [64, 768, 512], P('expert'), may hold values from -6 to 6
- w_gate: bfloat16 [64, 7168, 512], P('expert', 'dp'), may hold values from -0.25 to 0.25
- w_up: bfloat16 [64, 7168, 512], P('expert', 'dp'), may hold values from -0.25 to 0.25
- w_down: bfloat16 [64, 512, 7168], P('expert', None, 'dp'), may hold values from -0.0625 to 0.0625
Outputs:
- grad_tokens: bfloat16 [8192, 7168], P('expert', 'dp')
- grad_w_gate: bfloat16 [64, 7168, 512], P('expert', 'dp')
- grad_w_up: bfloat16 [64, 7168, 512], P('expert', 'dp')
- grad_w_down: bfloat16 [64, 512, 7168], P('expert', None, 'dp')
Inputs may be any that keep to these rules, and one draw needn't show every extreme that they name: `routes`: each row names 2 different experts. Within the 128 rows of one index of the expert axis no expert is named more than 12 times, and in some such block one expert is named exactly 12 times.
All inputs are finite; a program needn't handle non-finite values.
Results may differ from a plain program's by a relative error of at most 0.0072.
Values may be sent and summed in bfloat16 or wider, within the bound.
A program may use at most 32 MiB of HBM per device.

v0:
```python
import jax
import jax.numpy as jnp
from jax import lax
from jax.sharding import PartitionSpec as P


def contract(left, right, left_dim, right_dim):
    return lax.dot_general(
        left, right, (((left_dim,), (right_dim,)), ((), ())), preferred_element_type=jnp.float32
    )


def hidden_grads(back_hidden, gate_pre, up_pre):
    gate_value = gate_pre.astype(jnp.float32)
    up_value = up_pre.astype(jnp.float32)
    sigma = jax.nn.sigmoid(gate_value)
    gate_grad = (back_hidden * up_value * sigma * (1.0 + gate_value * (1.0 - sigma))).astype(
        jnp.bfloat16
    )
    up_grad = (back_hidden * gate_value * sigma).astype(jnp.bfloat16)
    return (gate_grad, up_grad)


def shards(tokens_in, grad_out, routes, gate_probs, saved_gate, saved_up, w_gate, w_up, w_down):
    groups = lax.axis_size("expert")
    experts = groups // 2
    top_count = routes.shape[1]
    features = grad_out.shape[1]
    slot_rows = saved_gate.shape[1]
    capacity = slot_rows // groups
    flat_routes = routes.reshape(-1)
    one_hot = (flat_routes[:, None] == jnp.arange(experts, dtype=jnp.int32)[None, :]).astype(
        jnp.int32
    )
    before = jnp.cumsum(one_hot, axis=0) - one_hot
    slot_index = jnp.sum(before * one_hot, axis=1)
    target = flat_routes * capacity + slot_index
    scaled = (gate_probs[:, :, None] * grad_out[:, None, :].astype(jnp.float32)).astype(
        jnp.bfloat16
    )
    scaled = scaled.reshape(-1, features)
    repeated = jnp.repeat(tokens_in, top_count, axis=0)
    send_in = jnp.zeros((experts * capacity, features), jnp.bfloat16).at[target].set(repeated)
    send_grad = jnp.zeros((experts * capacity, features), jnp.bfloat16).at[target].set(scaled)

    def duplicate(values):
        wide = jnp.broadcast_to(
            values.reshape(experts, 1, capacity, features), (experts, 2, capacity, features)
        )
        return wide.reshape(groups * capacity, features)

    rows_in, rows_grad = (
        lax.all_to_all(duplicate(send_in), "expert", split_axis=0, concat_axis=0, tiled=True),
        lax.all_to_all(duplicate(send_grad), "expert", split_axis=0, concat_axis=0, tiled=True),
    )
    gate_pre = saved_gate[0]
    up_pre = saved_up[0]
    weight_gate = w_gate[0]
    weight_up = w_up[0]
    weight_down = w_down[0]
    gate_value = gate_pre.astype(jnp.float32)
    activation = (gate_value * jax.nn.sigmoid(gate_value) * up_pre.astype(jnp.float32)).astype(
        jnp.bfloat16
    )
    grad_down = contract(activation, rows_grad, 0, 0)
    partial_hidden = contract(rows_grad, weight_down, 1, 1)
    back_hidden = lax.psum(partial_hidden, "dp")
    gate_grad, up_grad = hidden_grads(back_hidden, gate_pre, up_pre)
    grad_gate = contract(rows_in, gate_grad, 0, 0)
    grad_up = contract(rows_in, up_grad, 0, 0)
    input_grad = contract(gate_grad, weight_gate, 1, 1) + contract(up_grad, weight_up, 1, 1)
    block_grad = input_grad.astype(jnp.bfloat16)
    returned = lax.all_to_all(block_grad, "expert", split_axis=0, concat_axis=0, tiled=True)
    index_low = 2 * flat_routes * capacity + slot_index
    index_high = index_low + capacity
    pair_grad = (
        returned[index_low].astype(jnp.float32) + returned[index_high].astype(jnp.float32)
    ).astype(jnp.bfloat16)
    grad_tokens = jnp.sum(
        pair_grad.astype(jnp.float32).reshape(-1, top_count, features), axis=1
    ).astype(jnp.bfloat16)
    return (
        grad_tokens,
        grad_gate.astype(jnp.bfloat16)[None],
        grad_up.astype(jnp.bfloat16)[None],
        grad_down.astype(jnp.bfloat16)[None],
    )


def solution(mesh):
    return jax.shard_map(
        shards,
        mesh=mesh,
        in_specs=(
            P("expert", "dp"),
            P("expert", "dp"),
            P("expert", None),
            P("expert", None),
            P("expert", None, None),
            P("expert", None, None),
            P("expert", "dp", None),
            P("expert", "dp", None),
            P("expert", None, "dp"),
        ),
        out_specs=(
            P("expert", "dp"),
            P("expert", "dp", None),
            P("expert", "dp", None),
            P("expert", None, "dp"),
        ),
        check_vma=False,
    )
```

profile of v0, /device:TPU:8, one launch (start us, length us, event | category | flops | bytes accessed | tf_op | source)
XLA Modules:
  0.0 858.1 jit_solution(12260049330714411285)
XLA Ops:
  7.2 0.7 broadcast_multiply_fusion
  7.9 0.8 copy.26
  9.3 0.6 reduce-window.6
  10.3 0.8 copy.29
  11.3 1.0 copy.30
  12.5 0.4 mul.87
  13.0 1.7 scatter_custom_fusion
  14.8 1.1 broadcast_in_dim.34
  15.9 29.4 %all-to-all-start = ((bf16[64,12,448]{2,1,0:T(8,128)(2,1)}), bf16[64,12,448]{2,1,0:T(8,128)(2,1)S(1)}, u32[]{:S(2)}, u32[]{:S(2)}) async-start(bf16[64,12,448]{2,1,0:T(8,128)(2,1)} %bitcast.3), calls=%async_computation | async-start | bytes 2097152 | tf_op jit(solution)/shard_map/all_to_all | solution.py:54
  45.8 1.6 scatter_custom_fusion.1
  47.6 97.9 %all-to-all-done = bf16[64,12,448]{2,1,0:T(8,128)(2,1)S(1)} async-done(((bf16[64,12,448]{2,1,0:T(8,128)(2,1)}), bf16[64,12,448]{2,1,0:T(8,128)(2,1)S(1)}, u32[]{:S(2)}, u32[]{:S(2)}) %all-to-all-start) | async-done | bytes 688160 | tf_op jit(solution)/shard_map/all_to_all | solution.py:54
  145.5 1.1 broadcast_in_dim.37
  146.6 12.8 %all-to-all-start.2 = ((bf16[64,12,448]{2,1,0:T(8,128)(2,1)}), bf16[64,12,448]{2,1,0:T(8,128)(2,1)S(1)}, u32[]{:S(2)}, u32[]{:S(2)}) async-start(bf16[64,12,448]{2,1,0:T(8,128)(2,1)} %bitcast.89), calls=%async_computation.2 | async-start | bytes 2097152 | tf_op jit(solution)/shard_map/all_to_all | solution.py:53
  159.4 0.4 all_to_all.26
  159.9 1.7 fusion.26
  161.6 552.1 %all-reduce.2.cloned.1.call-done = f32[768,512]{1,0:T(8,128)} async-done(((f32[768,512]{1,0:T(8,128)}), f32[768,512]{1,0:T(8,128)}) %all-reduce.2.cloned.1.call-update) | async-done | bytes 1572880 | tf_op jit(solution)/shard_map/psum | solution.py:67
  713.8 2.4 fusion.13
  716.2 0.6 fusion.24
  717.6 1.4 fusion.17
  719.0 1.4 copy.31
  720.3 1.2 all_to_all.27
  721.6 24.9 %all-to-all-start.1 = ((bf16[64,12,448]{2,1,0:T(8,128)(2,1)}), bf16[64,12,448]{2,1,0:T(8,128)(2,1)S(1)}, u32[]{:S(2)}, u32[]{:S(2)}) async-start(bf16[64,12,448]{2,1,0:T(8,128)(2,1)} %all_to_all.27), calls=%async_computation.1 | async-start | bytes 2097152 | tf_op jit(solution)/shard_map/all_to_all | solution.py:73
  746.5 1.3 all_to_all.32
  747.8 3.1 fusion.20
  750.9 1.3 fusion.19
  752.2 1.3 fusion.18
  753.6 93.3 %all-to-all-done.1 = bf16[64,12,448]{2,1,0:T(8,128)(2,1)S(1)} async-done(((bf16[64,12,448]{2,1,0:T(8,128)(2,1)}), bf16[64,12,448]{2,1,0:T(8,128)(2,1)S(1)}, u32[]{:S(2)}, u32[]{:S(2)}) %all-to-all-start.1) | async-done | bytes 688160 | tf_op jit(solution)/shard_map/all_to_all | solution.py:73
  846.9 0.4 all_to_all.29
  847.3 1.2 gather_fusion.1
  848.5 1.2 gather_fusion
  849.8 0.7 reduce_sum.25
  850.5 0.8 copy.34
  (46 shorter events, 3.2 us)
Async XLA Ops:
  7.2 152.7 %copy-start = (bf16[1,512,448]{1,2,0:T(8,128)(2,1)S(1)}, bf16[1,512,448]{1,2,0:T(8,128)(2,1)}, u32[]{:S(2)}) copy-start(bf16[1,512,448]{1,2,0:T(8,128)(2,1)} %param.17) | copy-start | bytes 1376260
  14.8 30.6 %copy-start.9 = (bf16[128,448]{0,1:T(8,128)(2,1)S(1)}, bf16[128,448]{0,1:T(8,128)(2,1)}, u32[]{:S(2)}) copy-start(bf16[128,448]{0,1:T(8,128)(2,1)} %param.9) | copy-start | bytes 344068
  15.9 129.6 %all-to-all-start = ((bf16[64,12,448]{2,1,0:T(8,128)(2,1)}), bf16[64,12,448]{2,1,0:T(8,128)(2,1)S(1)}, u32[]{:S(2)}, u32[]{:S(2)}) async-start(bf16[64,12,448]{2,1,0:T(8,128)(2,1)} %bitcast.3), calls=%async_computation | async-start | bytes 2097152 | tf_op jit(solution)/shard_map/all_to_all | solution.py:54
  146.6 575.0 %all-to-all-start.2 = ((bf16[64,12,448]{2,1,0:T(8,128)(2,1)}), bf16[64,12,448]{2,1,0:T(8,128)(2,1)S(1)}, u32[]{:S(2)}, u32[]{:S(2)}) async-start(bf16[64,12,448]{2,1,0:T(8,128)(2,1)} %bitcast.89), calls=%async_computation.2 | async-start | bytes 2097152 | tf_op jit(solution)/shard_map/all_to_all | solution.py:53
  159.4 554.4 %all-reduce.2.cloned.1.call-start = ((), (), s32[]{:S(2)}) async-start(), calls=%async_computation.3 | async-start | bytes 3145728 | tf_op jit(solution)/shard_map/psum | solution.py:67
  159.9 553.9 %copy-start.5 = (bf16[1,768,512]{2,1,0:T(8,128)(2,1)S(1)}, bf16[1,768,512]{2,1,0:T(8,128)(2,1)}, u32[]{:S(2)}) copy-start(bf16[1,768,512]{2,1,0:T(8,128)(2,1)} %param.13) | copy-start | bytes 2359300
  161.6 554.6 %copy-start.7 = (bf16[1,448,512]{2,1,0:T(8,128)(2,1)S(1)}, bf16[1,448,512]{2,1,0:T(8,128)(2,1)}, u32[]{:S(2)}) copy-start(bf16[1,448,512]{2,1,0:T(8,128)(2,1)} %param.15) | copy-start | bytes 1376260
  716.2 0.9 copy-start.1
  716.2 1.2 copy-start.3
  716.2 1.4 copy-start.8
  721.6 125.3 %all-to-all-start.1 = ((bf16[64,12,448]{2,1,0:T(8,128)(2,1)}), bf16[64,12,448]{2,1,0:T(8,128)(2,1)S(1)}, u32[]{:S(2)}, u32[]{:S(2)}) async-start(bf16[64,12,448]{2,1,0:T(8,128)(2,1)} %all_to_all.27), calls=%async_computation.1 | async-start | bytes 2097152 | tf_op jit(solution)/shard_map/all_to_all | solution.py:73
  747.8 3.1 copy-start.4
  747.8 3.1 copy-start.6
  750.9 1.3 copy-start.2
Sparse Core Ops, SparseCore 0:
  163.8 549.9 all-reduce.1
where the time goes:
time: 859 us; the launch traced here: 858 us
  waiting for transfers between devices  743 us (86%)
  starting transfers between devices  67.2 us (8%)
  local copies, waits for them, and re-layouts  17.5 us (2%)
  between operations  14.3 us (2%)
  matrix products  9.4 us (1%)
    psum x1, waiting for transfers between devices, shards(): back_hidden = lax.psum(partial_hidden, 'dp')  552 us
    all_to_all x1, waiting for transfers between devices, shards(): lax.all_to_all(duplicate(send_grad), 'expert', split_axis=0, concat_axis=...  97.9 us
    all_to_all x1, waiting for transfers between devices, shards(): lax.all_to_all(block_grad, 'expert', split_axis=0, concat_axis=0, tiled=T...  93.3 us
    all_to_all x1, starting transfers between devices, shards(): lax.all_to_all(duplicate(send_grad), 'expert', split_axis=0, concat_axis=...  29.4 us
    all_to_all x1, starting transfers between devices, shards(): lax.all_to_all(block_grad, 'expert', split_axis=0, concat_axis=0, tiled=T...  24.9 us
  transfers between devices with their start and end apart: 4, of which 3 were waited for; matrix products, arithmetic and copies ran while one was open for 2% of the time, Pallas kernels for 0%

commit v1 on v0

v1 whole, which is shorter than its diff:
```python
import functools

import jax
import jax.numpy as jnp
from jax import lax
from jax.experimental import pallas as pl
from jax.experimental.pallas import tpu as pltpu
from jax.sharding import PartitionSpec as P

MESH = pl.DeviceIdType.MESH
Y = 4
CHUNKS = 4
BF = jnp.bfloat16
F32 = jnp.float32


def dot_nn(a, b):
    return lax.dot_general(a, b, (((1,), (0,)), ((), ())), preferred_element_type=F32)


def dot_nt(a, b):
    return lax.dot_general(a, b, (((1,), (1,)), ((), ())), preferred_element_type=F32)


def dot_tn(a, b):
    return lax.dot_general(a, b, (((0,), (0,)), ((), ())), preferred_element_type=F32)


def kernel(
    cfg,
    tok_t, grad_t, routes_t, probs_t, s_gate, s_up, w_gate, w_up, w_down_t,
    o_tok, o_gate, o_up, o_down,
    meta, r_tok, r_grad, r_meta, pack_b,
    sb1, sb2, x1, x2, wd, act,
    p32, pb, ra, q32, qb, rx, w32, wb, rz, hid,
    gg, ug, bg, rp, ps, rr, ot, ro,
    sem_ys, sem_yr, sem_z1s, sem_z1r, sem_f1s, sem_f1r, sem_z2s, sem_z2r, sem_f2s, sem_f2r,
    sem_as, sem_ar, sem_xs, sem_xr, sem_hs, sem_hr, sem_gs, sem_gr, sem_cs, sem_cr,
    sem_ps, sem_pr, sem_rs, sem_rr, sem_os, sem_or,
):
    nz, nx, nzh, cap, C = cfg
    G = nz // C
    feats, toks = tok_t.shape
    hidden = s_gate.shape[2]
    w1 = sb1.shape[2]
    msg = 2 * cap
    units = 2 * nx
    rows = 2 * G * msg

    e = lax.axis_index("expert")
    d = lax.axis_index("dp")
    y, z = e % Y, e // Y
    core, zh, x = d % 2, (d // 2) % nzh, d // (2 * nzh)
    par, h = y // 2, y % 2
    zq, zr = z // G, z % G
    pair = z * Y + (y + 1 - 2 * h)
    core_to = (x * nzh + zh) * 2 + (1 - core)
    zh_to = (x * nzh + (1 - zh)) * 2 + core

    def x_to(j):
        return (((x + j) % nx) * nzh + zh) * 2 + core

    def send_z(c, j):
        return ((zq + c) % C) * G + (zr + j) % G

    def recv_z(c, j):
        return ((zq + C - c) % C) * G + (zr + G - j) % G

    def group(c):
        return (zq + C - c) % C

    def remote(src, dst, ss, rs, ee, dd):
        return pltpu.make_async_remote_copy(
            src_ref=src, dst_ref=dst, send_sem=ss, recv_sem=rs,
            device_id=(ee, dd), device_id_type=MESH,
        )

    def loop(lo, hi, body):
        if hi - lo == 1:
            body(lo)
        elif hi > lo:
            lax.fori_loop(lo, hi, lambda i, _: (body(i), 0)[1], 0)

    barrier = pltpu.get_barrier_semaphore()

    def greet(ee, dd):
        pl.semaphore_signal(barrier, inc=1, device_id=(ee, dd), device_id_type=MESH)

    for j in range(1, Y):
        greet(z * Y + (y + j) % Y, d)
    loop(1, nz, lambda j: greet(((z + j) % nz) * Y + y, d))
    greet(e, core_to)
    for j in range(1, nx):
        greet(e, x_to(j))
    if nzh == 2:
        greet(e, zh_to)

    r0, r1 = routes_t[0:1, :], routes_t[1:2, :]
    eid = lax.broadcasted_iota(jnp.int32, (2 * nz, toks), 0)
    hit0, hit1 = (r0 == eid).astype(F32), (r1 == eid).astype(F32)
    upper = (
        lax.broadcasted_iota(jnp.int32, (toks, toks), 0) < lax.broadcasted_iota(jnp.int32, (toks, toks), 1)
    ).astype(BF)
    before = dot_nn((hit0 + hit1).astype(BF), upper)
    for k, (r, hit) in enumerate(((r0, hit0), (r1, hit1))):
        slot = jnp.sum(before * hit, axis=0, keepdims=True)
        meta[k : k + 1, :] = slot + ((r // 2) * msg).astype(F32)
        meta[2 + k : 3 + k, :] = (r % 2).astype(F32)
        meta[4 + k : 5 + k, :] = probs_t[k : k + 1, :]
    meta[6:8, :] = jnp.zeros((2, toks), F32)

    wd[0:feats, :] = w_down_t[...]
    wd[feats:, :] = jnp.zeros((w1 - feats, hidden), BF)

    pl.semaphore_wait(barrier, (Y - 1) + (nz - 1) + 1 + (nx - 1) + (1 if nzh == 2 else 0))

    sets = ((grad_t, r_grad), (meta, r_meta), (tok_t, r_tok))

    def y_copy(kind, j, i):
        src, dst = sets[kind]
        return remote(src, dst.at[i], sem_ys.at[kind * 2 + j], sem_yr.at[kind * 2 + i], z * Y + y // 2 + 2 * j, d)

    for j in range(2):
        to = y // 2 + 2 * j

        @pl.when(to != y)
        def _():
            for kind in range(3):
                y_copy(kind, j, h).start()

        @pl.when(to == y)
        def _():
            for src, dst in sets:
                dst[h] = src[...]

    for i in range(2):
        @pl.when(2 * h + i != y)
        def _():
            for kind in range(3):
                y_copy(kind, 0, i).wait_recv()

    targets = []
    parity = par.astype(F32)
    for k in range(2):
        for i in range(2):
            t = r_meta[i, k : k + 1, :] + float(cap * i)
            targets.append(jnp.where(r_meta[i, 2 + k : 3 + k, :] == parity, t, -1.0))
            lanes = pl.ds((2 * k + i) * toks, toks)
            scaled = r_grad[i].astype(F32) * r_meta[i, 4 + k : 5 + k, :]
            pack_b[0:feats, lanes] = scaled.astype(BF)
            pack_b[feats : 2 * feats, lanes] = r_tok[i]

    def z1_copy(c, j):
        to = send_z(c, j)
        return remote(sb1.at[to], x1.at[2 * z + h], sem_z1s.at[c * G + j], sem_z1r.at[c * G + j], to * Y + y, d)

    def z2_copy(c, j):
        to = send_z(c, j)
        return remote(sb2.at[to], x2.at[2 * z + h], sem_z2s.at[c * G + j], sem_z2r.at[c * G + j], to * Y + y, d)

    def f1_copy(c, j):
        at = 2 * recv_z(c, j) + h
        return remote(x1.at[at], x1.at[at], sem_f1s.at[c * G + j], sem_f1r.at[c * G + j], pair, d)

    def f2_copy(c, j):
        at = 2 * recv_z(c, j) + h
        return remote(x2.at[at], x2.at[at], sem_f2s.at[c * G + j], sem_f2r.at[c * G + j], pair, d)

    def first(c):
        return 1 if c == 0 else 0

    def pack(c):
        g = (zq + c) % C
        base = (g * (G * msg)).astype(F32)
        ids = lax.broadcasted_iota(jnp.int32, (G * msg, toks), 0).astype(F32) + base
        one_hot = jnp.concatenate([(t == ids).astype(BF) for t in targets], axis=1)
        packed = dot_nt(one_hot, pack_b[...]).astype(BF).reshape(G, msg, 2 * feats)
        sb1[pl.ds(g * G, G)] = packed[:, :, 0:w1]
        sb2[pl.ds(g * G, G)] = packed[:, :, w1:]
        if c == 0:
            x1[2 * z + h] = sb1[z]
            x2[2 * z + h] = sb2[z]
            f1_copy(0, 0).start()
        loop(first(c), G, lambda j: z1_copy(c, j).start())

    for c in range(C):
        pack(c)

    def activate(i):
        gv = s_gate[i].astype(F32)
        act[i] = (gv * jax.nn.sigmoid(gv) * s_up[i].astype(F32)).astype(BF)

    loop(0, 2 * nz, activate)

    def send_second(c):
        if c == 0:
            f2_copy(0, 0).start()
        loop(first(c), G, lambda j: z2_copy(c, j).start())

    def a_copy(c):
        return remote(pb.at[c, pl.ds((1 - core) * nx, nx)], ra.at[c], sem_as.at[c], sem_ar.at[c], e, core_to)

    def x_copy(c, j):
        k = c * (nx - 1) + j - 1
        return remote(qb.at[c, (x + j) % nx], rx.at[c, j - 1], sem_xs.at[k], sem_xr.at[k], e, x_to(j))

    def h_copy(c):
        return remote(wb.at[c], rz.at[c], sem_hs.at[c], sem_hr.at[c], e, zh_to)

    def g_copy(c, j):
        k = c * (nx - 1) + j - 1
        at = core * nx + x
        return remote(hid.at[c, at], hid.at[c, at], sem_gs.at[k], sem_gr.at[k], e, x_to(j))

    def c_copy(c):
        half = hid.at[c, pl.ds(core * nx, nx)]
        return remote(half, half, sem_cs.at[c], sem_cr.at[c], e, core_to)

    def p_copy(c):
        g = group(c)
        return remote(bg.at[1 - h, pl.ds(g * G, G)], rp.at[pl.ds(g * G, G)], sem_ps.at[c], sem_pr.at[c], pair, d)

    def r_copy(c, j):
        to = recv_z(c, j)
        return remote(ps.at[to], rr.at[z], sem_rs.at[c * G + j], sem_rr.at[c * G + j], to * Y + y, d)

    def stage_forward(c):
        def body(j):
            z1_copy(c, j).wait_recv()
            f1_copy(c, j).start()

        loop(first(c), G, body)

    def stage_product(c):
        loop(0, G, lambda j: f1_copy(c, j).wait_recv())
        g = group(c)
        left = x1[pl.ds(2 * G * g, 2 * G)].reshape(rows, w1)
        part = dot_nn(left, wd[...]).reshape(units, rows // units, hidden)
        p32[c] = part
        pb[c] = part.astype(BF)
        a_copy(c).start()

    def stage_core(c):
        a_copy(c).wait_recv()
        total = p32[c, pl.ds(core * nx, nx)] + ra[c].astype(F32)
        q32[c] = total
        qb[c] = total.astype(BF)
        for j in range(1, nx):
            x_copy(c, j).start()

    def stage_x(c):
        for j in range(1, nx):
            x_copy(c, j).wait_recv()
        total = q32[c, x]
        for j in range(1, nx):
            total = total + rx[c, j - 1].astype(F32)
        w32[c] = total
        wb[c] = total.astype(BF)
        if nzh == 2:
            h_copy(c).start()

    def stage_zh(c):
        total = w32[c]
        if nzh == 2:
            h_copy(c).wait_recv()
            total = total + rz[c].astype(F32)
        hid[c, core * nx + x] = total.astype(BF)
        for j in range(1, nx):
            g_copy(c, j).start()

    def stage_gather(c):
        for j in range(1, nx):
            g_copy(c, j).wait_recv()
        c_copy(c).start()

    def stage_hidden(c):
        c_copy(c).wait_recv()
        g = group(c)
        at = pl.ds(2 * G * g, 2 * G)
        back = hid[c].astype(F32).reshape(rows, hidden)
        gv = s_gate[at].astype(F32).reshape(rows, hidden)
        uv = s_up[at].astype(F32).reshape(rows, hidden)
        sig = jax.nn.sigmoid(gv)
        g_grad = (back * uv * sig * (1.0 + gv * (1.0 - sig))).astype(BF)
        u_grad = (back * gv * sig).astype(BF)
        gg[at] = g_grad.reshape(2 * G, msg, hidden)
        ug[at] = u_grad.reshape(2 * G, msg, hidden)
        block = (dot_nt(g_grad, w_gate[...]) + dot_nt(u_grad, w_up[...])).astype(BF)
        block = block.reshape(G, 2, msg, feats)
        bg[0, pl.ds(g * G, G)] = block[:, 0]
        bg[1, pl.ds(g * G, G)] = block[:, 1]
        p_copy(c).start()

    def stage_pair(c):
        p_copy(c).wait_recv()
        at = pl.ds(group(c) * G, G)
        ps[at] = (bg[h, at].astype(F32) + rp[at].astype(F32)).astype(BF)
        if c == 0:
            rr[z] = ps[z]
        loop(first(c), G, lambda j: r_copy(c, j).start())

    def stage_second(c):
        send_second(c)

    stages = [
        stage_forward, stage_product, stage_core, stage_x, stage_second, stage_zh,
        stage_gather, stage_hidden, stage_pair,
    ]
    for step in range(C + len(stages) - 1):
        for s in reversed(range(len(stages))):
            c = step - s
            if 0 <= c < C:
                stages[s](c)

    for c in range(C):
        def forward2(j):
            z2_copy(c, j).wait_recv()
            f2_copy(c, j).start()

        loop(first(c), G, forward2)

    total_rows = 2 * nz * msg
    right = act[...].reshape(total_rows, hidden)
    for m in range(w1 // 128):
        lo, hi = m * 128, min((m + 1) * 128, feats)
        left = x1[:, :, m * 128 : (m + 1) * 128].reshape(total_rows, 128)
        o_down[lo:hi, :] = dot_tn(left, right)[0 : hi - lo].astype(BF)

    for c in range(C):
        loop(0, G, lambda j: f2_copy(c, j).wait_recv())
    skip = 128 - (w1 - feats)
    for grads, out in ((gg, o_gate), (ug, o_up)):
        right = grads[...].reshape(total_rows, hidden)
        left = x1[:, :, w1 - 128 : w1].reshape(total_rows, 128)
        out[0 : 128 - skip, :] = dot_tn(left, right)[skip:].astype(BF)
        for m in range((2 * feats - w1) // 128):
            left = x2[:, :, m * 128 : (m + 1) * 128].reshape(total_rows, 128)
            lo = 128 - skip + m * 128
            out[lo : lo + 128, :] = dot_tn(left, right).astype(BF)

    for c in range(C):
        loop(first(c), G, lambda j: r_copy(c, j).wait_recv())
    ids = lax.broadcasted_iota(jnp.int32, (nz * msg, toks), 0).astype(F32)
    back_rows = rr[...].reshape(nz * msg, feats)

    def o_copy(i, j):
        return remote(ot.at[i], ro.at[par], sem_os.at[i], sem_or.at[j], z * Y + 2 * h + i, d)

    for i in range(2):
        pick = ((targets[i] == ids).astype(F32) + (targets[2 + i] == ids).astype(F32)).astype(BF)
        ot[i] = dot_tn(back_rows, pick).astype(BF)
        s = 2 * h + i

        for p in range(2):
            @pl.when((s != y) & (par == p))
            def _():
                o_copy(i, p).start()

        @pl.when(s == y)
        def _():
            ro[par] = ot[i]

    for j in range(2):
        @pl.when(y // 2 + 2 * j != y)
        def _():
            o_copy(0, j).wait_recv()

    o_tok[...] = (ro[0].astype(F32) + ro[1].astype(F32)).astype(BF)

    for j in range(2):
        @pl.when(y // 2 + 2 * j != y)
        def _():
            for kind in range(3):
                y_copy(kind, j, h).wait_send()

    for c in range(C):
        def sent(j):
            z1_copy(c, j).wait_send()
            z2_copy(c, j).wait_send()
            r_copy(c, j).wait_send()

        loop(first(c), G, sent)

        def forwarded(j):
            f1_copy(c, j).wait_send()
            f2_copy(c, j).wait_send()

        loop(0, G, forwarded)
        a_copy(c).wait_send()
        for j in range(1, nx):
            x_copy(c, j).wait_send()
            g_copy(c, j).wait_send()
        if nzh == 2:
            h_copy(c).wait_send()
        c_copy(c).wait_send()
        p_copy(c).wait_send()
    for i in range(2):
        @pl.when(2 * h + i != y)
        def _():
            o_copy(i, 0).wait_send()


def shards(dp_shape, chunks, tokens_in, grad_out, routes, gate_probs, saved_gate, saved_up, w_gate, w_up, w_down):
    groups = lax.axis_size("expert")
    nx, nzh = dp_shape
    nz = groups // Y
    slot_rows, hidden = saved_gate.shape[1:]
    cap = slot_rows // groups
    toks, feats = tokens_in.shape
    msg = 2 * cap
    C = chunks
    G = nz // C
    w1 = -(-feats // 128) * 128
    w2 = 2 * feats - w1
    units = 2 * nx
    unit = 2 * G * msg // units
    dma = lambda n: pltpu.SemaphoreType.DMA((n,))
    vm = lambda shape, dtype=BF: pltpu.VMEM(shape, dtype)
    scratch = [
        vm((8, toks), F32), vm((2, feats, toks)), vm((2, feats, toks)), vm((2, 8, toks), F32),
        vm((2 * feats, 4 * toks)),
        vm((nz, msg, w1)), vm((nz, msg, w2)), vm((2 * nz, msg, w1)), vm((2 * nz, msg, w2)),
        vm((w1, hidden)), vm((2 * nz, msg, hidden)),
        vm((C, units, unit, hidden), F32), vm((C, units, unit, hidden)), vm((C, nx, unit, hidden)),
        vm((C, nx, unit, hidden), F32), vm((C, nx, unit, hidden)), vm((C, max(nx - 1, 1), unit, hidden)),
        vm((C, unit, hidden), F32), vm((C, unit, hidden)), vm((C, unit, hidden)),
        vm((C, units, unit, hidden)),
        vm((2 * nz, msg, hidden)), vm((2 * nz, msg, hidden)),
        vm((2, nz, msg, feats)), vm((nz, msg, feats)), vm((nz, msg, feats)), vm((nz, msg, feats)),
        vm((2, feats, toks)), vm((2, feats, toks)),
        dma(6), dma(6), dma(nz), dma(nz), dma(nz), dma(nz), dma(nz), dma(nz), dma(nz), dma(nz),
        dma(C), dma(C), dma(C * max(nx - 1, 1)), dma(C * max(nx - 1, 1)), dma(C), dma(C),
        dma(C * max(nx - 1, 1)), dma(C * max(nx - 1, 1)), dma(C), dma(C),
        dma(C), dma(C), dma(nz), dma(nz), dma(2), dma(2),
    ]
    o_tok, o_gate, o_up, o_down = pl.pallas_call(
        functools.partial(kernel, (nz, nx, nzh, cap, C)),
        out_shape=(
            jax.ShapeDtypeStruct((feats, toks), BF),
            jax.ShapeDtypeStruct((feats, hidden), BF),
            jax.ShapeDtypeStruct((feats, hidden), BF),
            jax.ShapeDtypeStruct((feats, hidden), BF),
        ),
        in_specs=[pl.BlockSpec(memory_space=pltpu.VMEM)] * 9,
        out_specs=(pl.BlockSpec(memory_space=pltpu.VMEM),) * 4,
        scratch_shapes=scratch,
        compiler_params=pltpu.CompilerParams(
            collective_id=0, has_side_effects=True, vmem_limit_bytes=48 * 1024 * 1024
        ),
    )(
        tokens_in.T, grad_out.T, routes.T, gate_probs.T,
        saved_gate.reshape(2 * nz, msg, hidden), saved_up.reshape(2 * nz, msg, hidden),
        w_gate[0], w_up[0], w_down[0].T,
    )
    return o_tok.T, o_gate[None], o_up[None], o_down.T[None]


def build(mesh, dp_shape, chunks):
    return jax.shard_map(
        functools.partial(shards, dp_shape, chunks),
        mesh=mesh,
        in_specs=(
            P("expert", "dp"),
            P("expert", "dp"),
            P("expert", None),
            P("expert", None),
            P("expert", None, None),
            P("expert", None, None),
            P("expert", "dp", None),
            P("expert", "dp", None),
            P("expert", None, "dp"),
        ),
        out_specs=(
            P("expert", "dp"),
            P("expert", "dp", None),
            P("expert", "dp", None),
            P("expert", None, "dp"),
        ),
        check_vma=False,
    )


def solution(mesh):
    return build(mesh, (4, 2), CHUNKS)
```

time: 859 us -> 181 us (0.21)
  the two profiles are of different devices: /device:TPU:8 before, /device:TPU:192 now
where the time goes in v1:
time: 181 us
  Pallas kernels  170 us (94%)
  local copies, waits for them, and re-layouts  10.7 us (6%)
    pallas_call x1, Pallas kernels, shards(): pl.pallas_call(functools.partial(kernel, (nz, nx, nzh, cap, C)), out_shap...  170 us
    unnamed x22, local copies, waits for them, and re-layouts  10.7 us

profile of v1, /device:TPU:192, one launch (start us, length us, event | category | flops | bytes accessed | tf_op | source)
XLA Modules:
  0.0 181.1 jit_solution(7609723174203002058)
XLA Ops:
  0.6 0.0 copy-start.8
  0.6 0.0 copy-start.7
  0.7 0.7 copy-done.8
  1.3 0.0 copy-done.7
  1.3 0.0 copy-start
  1.3 1.1 copy-done
  2.5 0.0 copy-start.1
  2.5 1.1 copy-done.1
  3.6 0.0 copy-start.2
  3.6 1.0 copy-done.2
  4.6 0.0 copy-start.3
  4.6 1.0 copy-done.3
  5.6 0.0 copy-start.4
  5.6 1.0 copy-done.4
  6.7 0.0 copy-start.5
  6.7 0.9 copy-done.5
  7.6 0.0 copy-start.6
  7.6 0.9 copy-done.6
  8.5 169.6 %shard_map.120 = (bf16[448,128]{1,0:T(8,128)(2,1)S(1)}, bf16[448,512]{1,0:T(8,128)(2,1)S(1)}, bf16[448,512]{1,0:T(8,128)(2,1)S(1)}, bf16[448,512]{1,0:T(8,128)(2,1)S(1)}) custom-call(bf16[448,128]{1,0:T(8,128)(2,1)S(1)} %bitcast.26, bf16[448,128]{1,0:T(8,128)(2,1)S(1)} %bitcast.27, s32[2,128]{1,0:T(2,128)S(1)} %bitcast.28, f32[2,128]{1,0:T(2,128)S(1)} %bitcast.29, ...), custom_call_target="tpu_custom_call" | custom-call | tf_op jit(solution)/shard_map/pallas_call | solution.py:436
  178.1 0.6 copy.17
  178.8 0.8 copy.18
  179.5 0.8 copy.19
  180.3 0.8 copy.20
Async XLA Ops:
  0.6 0.7 copy-start.8
  0.6 0.7 copy-start.7
  1.3 1.1 copy-start
  2.5 1.1 copy-start.1
  3.6 1.0 copy-start.2
  4.6 1.0 copy-start.3
  5.6 1.0 copy-start.4
  6.7 0.9 copy-start.5
  7.6 0.9 copy-start.6

commit v2 on v1

v2 whole, which is shorter than its diff:
```python
import functools

import jax
import jax.numpy as jnp
from jax import lax
from jax.experimental import pallas as pl
from jax.experimental.pallas import tpu as pltpu
from jax.sharding import PartitionSpec as P

MESH = pl.DeviceIdType.MESH
Y = 4
CHUNKS = 2
BF = jnp.bfloat16
F32 = jnp.float32


def dot_nn(a, b):
    return lax.dot_general(a, b, (((1,), (0,)), ((), ())), preferred_element_type=F32)


def dot_nt(a, b):
    return lax.dot_general(a, b, (((1,), (1,)), ((), ())), preferred_element_type=F32)


def dot_tn(a, b):
    return lax.dot_general(a, b, (((0,), (0,)), ((), ())), preferred_element_type=F32)


def kernel(
    cfg,
    tok_t, grad_t, routes_t, probs_t, h_gate, h_up, h_wg, h_wu, h_wd,
    o_tok, o_gate, o_up, o_down,
    s_gate, s_up, w_gate, w_up, sem_in,
    meta, r_tok, r_grad, r_meta, pack_b, pack_c,
    sb1, sb2, x1, x2, wd, act,
    p32, pb, rx, w32, wb, rz, hid,
    xt, wt, out32, gg, ug, bg, rp, ps, rr, ot, ro,
    sem_ys, sem_yr, sem_z1s, sem_z1r, sem_f1s, sem_f1r, sem_z2s, sem_z2r, sem_f2s, sem_f2r,
    sem_xs, sem_xr, sem_hs, sem_hr, sem_gs, sem_gr,
    sem_ps, sem_pr, sem_rs, sem_rr, sem_os, sem_or,
):
    nz, nx, nzh, cap, C = cfg
    G = nz // C
    feats, toks = tok_t.shape
    hidden = h_gate.shape[2]
    w1 = sb1.shape[2]
    msg = 2 * cap
    units = 2 * nx
    rows = 2 * G * msg

    e = lax.axis_index("expert")
    d = lax.axis_index("dp")
    y, z = lax.rem(e, Y), lax.div(e, Y)
    core, zh, x = lax.rem(d, 2), lax.rem(lax.div(d, 2), nzh), lax.div(d, 2 * nzh)
    par, h = lax.div(y, 2), lax.rem(y, 2)
    zq, zr = lax.div(z, G), lax.rem(z, G)
    pair = z * Y + (y + 1 - 2 * h)
    me = core * nx + x
    zh_to = (x * nzh + (1 - zh)) * 2 + core

    def dp_to(j):
        v = lax.rem(me + j, units)
        return (lax.rem(v, nx) * nzh + zh) * 2 + lax.div(v, nx)

    def send_z(c, j):
        return lax.rem(zq + c, C) * G + lax.rem(zr + j, G)

    def recv_z(c, j):
        return lax.rem(zq + (C - c), C) * G + lax.rem(zr + G - j, G)

    def group(c):
        return lax.rem(zq + (C - c), C)

    def remote(src, dst, ss, rs, ee, dd):
        return pltpu.make_async_remote_copy(
            src_ref=src, dst_ref=dst, send_sem=ss, recv_sem=rs,
            device_id=(ee, dd), device_id_type=MESH,
        )

    def loop(lo, hi, body):
        if hi - lo == 1:
            body(lo)
        elif hi > lo:
            lax.fori_loop(lo, hi, lambda i, _: (body(i), 0)[1], 0)

    ins = [
        pltpu.make_async_copy(src, dst, sem_in.at[n])
        for n, (src, dst) in enumerate(
            ((h_gate, s_gate), (h_up, s_up), (h_wd, wd.at[0:feats]), (h_wg, w_gate), (h_wu, w_up))
        )
    ]
    for copy in ins:
        copy.start()
    wd[feats:, :] = jnp.zeros((w1 - feats, hidden), BF)

    barrier = pltpu.get_barrier_semaphore()

    def greet(ee, dd):
        pl.semaphore_signal(barrier, inc=1, device_id=(ee, dd), device_id_type=MESH)

    for j in range(1, Y):
        greet(z * Y + (y + j) % Y, d)
    loop(1, nz, lambda j: greet(lax.rem(z + j, nz) * Y + y, d))
    loop(1, units, lambda j: greet(e, dp_to(j)))
    if nzh == 2:
        greet(e, zh_to)

    r0, r1 = routes_t[0:1, :], routes_t[1:2, :]
    eid = lax.broadcasted_iota(jnp.int32, (2 * nz, toks), 0)
    hit0, hit1 = (r0 == eid).astype(F32), (r1 == eid).astype(F32)
    upper = (
        lax.broadcasted_iota(jnp.int32, (toks, toks), 0) < lax.broadcasted_iota(jnp.int32, (toks, toks), 1)
    ).astype(BF)
    before = dot_nn((hit0 + hit1).astype(BF), upper)
    for k, (r, hit) in enumerate(((r0, hit0), (r1, hit1))):
        slot = jnp.sum(before * hit, axis=0, keepdims=True)
        meta[k : k + 1, :] = slot + ((r // 2) * msg).astype(F32)
        meta[2 + k : 3 + k, :] = (r % 2).astype(F32)
        meta[4 + k : 5 + k, :] = probs_t[k : k + 1, :]
    meta[6:8, :] = jnp.zeros((2, toks), F32)

    pl.semaphore_wait(barrier, (Y - 1) + (nz - 1) + (units - 1) + (1 if nzh == 2 else 0))

    lead = w1 - feats
    sets = (
        (grad_t, lambda i: r_grad.at[i]),
        (meta, lambda i: r_meta.at[i]),
        (tok_t.at[0:lead], lambda i: r_tok.at[i, 0:lead]),
        (tok_t.at[lead:feats], lambda i: r_tok.at[i, lead:feats]),
    )

    def y_copy(kind, j, i):
        src, dst = sets[kind]
        return remote(src, dst(i), sem_ys.at[kind * 2 + j], sem_yr.at[kind * 2 + i], z * Y + y // 2 + 2 * j, d)

    for j in range(2):
        to = y // 2 + 2 * j

        @pl.when(to != y)
        def _():
            for kind in range(4):
                y_copy(kind, j, h).start()

        @pl.when(to == y)
        def _():
            r_grad[h] = grad_t[...]
            r_meta[h] = meta[...]
            r_tok[h] = tok_t[...]

    for i in range(2):
        @pl.when(2 * h + i != y)
        def _():
            for kind in range(3):
                y_copy(kind, 0, i).wait_recv()

    targets = []
    parity = par.astype(F32)
    for k in range(2):
        for i in range(2):
            t = r_meta[i, k : k + 1, :] + float(cap * i)
            targets.append(jnp.where(r_meta[i, 2 + k : 3 + k, :] == parity, t, -1.0))
            lanes = pl.ds((2 * k + i) * toks, toks)
            scaled = r_grad[i].astype(F32) * r_meta[i, 4 + k : 5 + k, :]
            both = jnp.concatenate([scaled.astype(BF), r_tok[i, 0:lead]], axis=0)
            pack_b[lanes, :] = both.T

    def z1_copy(c, j):
        to = send_z(c, j)
        return remote(sb1.at[to], x1.at[2 * z + h], sem_z1s.at[c * G + j], sem_z1r.at[c * G + j], to * Y + y, d)

    def z2_copy(c, j):
        to = send_z(c, j)
        return remote(sb2.at[to], x2.at[2 * z + h], sem_z2s.at[c * G + j], sem_z2r.at[c * G + j], to * Y + y, d)

    def f1_copy(c, j):
        at = 2 * recv_z(c, j) + h
        return remote(x1.at[at], x1.at[at], sem_f1s.at[c * G + j], sem_f1r.at[c * G + j], pair, d)

    def f2_copy(c, j):
        at = 2 * recv_z(c, j) + h
        return remote(x2.at[at], x2.at[at], sem_f2s.at[c * G + j], sem_f2r.at[c * G + j], pair, d)

    def first(c):
        return 1 if c == 0 else 0

    def pack(c):
        g = lax.rem(zq + c, C)
        base = (g * (G * msg)).astype(F32)
        ids = lax.broadcasted_iota(jnp.int32, (G * msg, toks), 0).astype(F32) + base
        one_hot = jnp.concatenate([(t == ids).astype(BF) for t in targets], axis=1)
        sb1[pl.ds(g * G, G)] = dot_nn(one_hot, pack_b[...]).astype(BF).reshape(G, msg, w1)
        if c == 0:
            x1[2 * z + h] = sb1[z]
            f1_copy(0, 0).start()
        loop(first(c), G, lambda j: z1_copy(c, j).start())

    for c in range(C):
        pack(c)

    for copy in ins:
        copy.wait()

    total_rows = 2 * nz * msg

    def fill_weights():
        for n, ref in enumerate((w_gate, w_up)):
            wt[n * hidden : (n + 1) * hidden, :] = ref[...].T

    def fill_activation():
        def body(i):
            gv = s_gate[i].astype(F32)
            act[i] = (gv * jax.nn.sigmoid(gv) * s_up[i].astype(F32)).astype(BF)

        loop(0, 2 * nz, body)

    def turn(ref, lo):
        for m in range(ref.shape[2] // 128):
            at = lo + m * 128
            xt[at : at + 128, :] = ref[:, :, m * 128 : (m + 1) * 128].reshape(total_rows, 128).T

    def fill_down():
        turn(x1, 0)
        o_down[...] = dot_nn(xt[0:feats, :], act[...].reshape(total_rows, hidden)).astype(BF)

    def fill_second():
        for i in range(2):
            @pl.when(2 * h + i != y)
            def _():
                y_copy(3, 0, i).wait_recv()

        for i in range(2):
            pack_c[i * toks : (i + 1) * toks, :] = r_tok[i, lead:feats].T

    def picks(c):
        g = lax.rem(zq + c, C)
        ids = lax.broadcasted_iota(jnp.int32, (G * msg, toks), 0).astype(F32) + (g * (G * msg)).astype(F32)
        both = [((targets[i] == ids).astype(F32) + (targets[2 + i] == ids).astype(F32)).astype(BF) for i in range(2)]
        return g, jnp.concatenate(both, axis=1)

    def send_second(c):
        g, one_hot = picks(c)
        sb2[pl.ds(g * G, G)] = dot_nn(one_hot, pack_c[...]).astype(BF).reshape(G, msg, 2 * feats - w1)
        if c == 0:
            x2[2 * z + h] = sb2[z]
            f2_copy(0, 0).start()
        loop(first(c), G, lambda j: z2_copy(c, j).start())

    def x_copy(c, j):
        k = c * (units - 1) + j - 1
        return remote(pb.at[c, lax.rem(me + j, units)], rx.at[c, j - 1], sem_xs.at[k], sem_xr.at[k], e, dp_to(j))

    def h_copy(c):
        return remote(wb.at[c], rz.at[c], sem_hs.at[c], sem_hr.at[c], e, zh_to)

    def g_copy(c, j):
        k = c * (units - 1) + j - 1
        return remote(hid.at[c, me], hid.at[c, me], sem_gs.at[k], sem_gr.at[k], e, dp_to(j))

    def p_copy(c):
        g = group(c)
        return remote(bg.at[1 - h, pl.ds(g * G, G)], rp.at[pl.ds(g * G, G)], sem_ps.at[c], sem_pr.at[c], pair, d)

    def r_copy(c, j):
        to = recv_z(c, j)
        return remote(ps.at[to], rr.at[z], sem_rs.at[c * G + j], sem_rr.at[c * G + j], to * Y + y, d)

    def stage_forward(c):
        def body(j):
            z1_copy(c, j).wait_recv()
            f1_copy(c, j).start()

        loop(first(c), G, body)

    def stage_product(c):
        loop(0, G, lambda j: f1_copy(c, j).wait_recv())
        g = group(c)
        left = x1[pl.ds(2 * G * g, 2 * G)].reshape(rows, w1)
        part = dot_nn(left, wd[...]).reshape(units, rows // units, hidden)
        p32[c] = part
        pb[c] = part.astype(BF)
        loop(1, units, lambda j: x_copy(c, j).start())

    def stage_sum(c):
        loop(1, units, lambda j: x_copy(c, j).wait_recv())
        total = p32[c, me]
        for j in range(1, units):
            total = total + rx[c, j - 1].astype(F32)
        w32[c] = total
        if nzh == 2:
            wb[c] = total.astype(BF)
            h_copy(c).start()

    def stage_zh(c):
        total = w32[c]
        if nzh == 2:
            h_copy(c).wait_recv()
            total = total + rz[c].astype(F32)
        hid[c, me] = total.astype(BF)
        loop(1, units, lambda j: g_copy(c, j).start())

    def stage_hidden(c):
        loop(1, units, lambda j: g_copy(c, j).wait_recv())
        g = group(c)
        at = pl.ds(2 * G * g, 2 * G)
        back = hid[c].astype(F32).reshape(rows, hidden)
        gv = s_gate[at].astype(F32).reshape(rows, hidden)
        uv = s_up[at].astype(F32).reshape(rows, hidden)
        sig = jax.nn.sigmoid(gv)
        g_grad = (back * uv * sig * (1.0 + gv * (1.0 - sig))).astype(BF)
        u_grad = (back * gv * sig).astype(BF)
        joined = jnp.concatenate([g_grad, u_grad], axis=1)
        gg[at] = g_grad.reshape(2 * G, msg, hidden)
        ug[at] = u_grad.reshape(2 * G, msg, hidden)
        block = dot_nn(joined, wt[...]).astype(BF).reshape(G, 2, msg, feats)
        bg[0, pl.ds(g * G, G)] = block[:, 0]
        bg[1, pl.ds(g * G, G)] = block[:, 1]
        p_copy(c).start()

    def stage_pair(c):
        p_copy(c).wait_recv()
        at = pl.ds(group(c) * G, G)
        ps[at] = (bg[h, at].astype(F32) + rp[at].astype(F32)).astype(BF)
        if c == 0:
            rr[z] = ps[z]
        loop(first(c), G, lambda j: r_copy(c, j).start())

    def stage_second(c):
        send_second(c)

    stages = [stage_forward, stage_product, stage_sum, stage_second, stage_zh, stage_hidden, stage_pair]
    fillers = {0: fill_second, 1: fill_weights, 2: fill_activation, C + 1: fill_down}
    for step in range(C + len(stages) - 1):
        for s in reversed(range(len(stages))):
            c = step - s
            if 0 <= c < C:
                stages[s](c)
        if step in fillers:
            fillers[step]()

    for c in range(C):
        def forward2(j):
            z2_copy(c, j).wait_recv()
            f2_copy(c, j).start()

        loop(first(c), G, forward2)

    for c in range(C):
        loop(0, G, lambda j: f2_copy(c, j).wait_recv())
    turn(x2, w1)
    for grads, out in ((gg, o_gate), (ug, o_up)):
        out[...] = dot_nn(xt[feats : 2 * feats, :], grads[...].reshape(total_rows, hidden)).astype(BF)

    for c in range(C):
        loop(first(c), G, lambda j: r_copy(c, j).wait_recv())
        g, one_hot = picks(c)
        back_rows = rr[pl.ds(g * G, G)].reshape(G * msg, feats)
        part = dot_tn(back_rows, one_hot)
        out32[...] = part if c == 0 else out32[...] + part

    def o_copy(i, j):
        return remote(ot.at[i], ro.at[par], sem_os.at[i], sem_or.at[j], z * Y + 2 * h + i, d)

    for i in range(2):
        ot[i] = out32[:, i * toks : (i + 1) * toks].astype(BF)
        s = 2 * h + i

        for p in range(2):
            @pl.when((s != y) & (par == p))
            def _():
                o_copy(i, p).start()

        @pl.when(s == y)
        def _():
            ro[par] = ot[i]

    for j in range(2):
        @pl.when(y // 2 + 2 * j != y)
        def _():
            o_copy(0, j).wait_recv()

    o_tok[...] = (ro[0].astype(F32) + ro[1].astype(F32)).astype(BF)

    for j in range(2):
        @pl.when(y // 2 + 2 * j != y)
        def _():
            for kind in range(4):
                y_copy(kind, j, h).wait_send()

    for c in range(C):
        def sent(j):
            z1_copy(c, j).wait_send()
            z2_copy(c, j).wait_send()
            r_copy(c, j).wait_send()

        loop(first(c), G, sent)

        def forwarded(j):
            f1_copy(c, j).wait_send()
            f2_copy(c, j).wait_send()

        loop(0, G, forwarded)
        loop(1, units, lambda j: (x_copy(c, j).wait_send(), g_copy(c, j).wait_send()))
        if nzh == 2:
            h_copy(c).wait_send()
        p_copy(c).wait_send()
    for i in range(2):
        @pl.when(2 * h + i != y)
        def _():
            o_copy(i, 0).wait_send()


def shards(dp_shape, chunks, tokens_in, grad_out, routes, gate_probs, saved_gate, saved_up, w_gate, w_up, w_down):
    groups = lax.axis_size("expert")
    nx, nzh = dp_shape
    nz = groups // Y
    slot_rows, hidden = saved_gate.shape[1:]
    cap = slot_rows // groups
    toks, feats = tokens_in.shape
    msg = 2 * cap
    C = chunks
    G = nz // C
    w1 = -(-feats // 128) * 128
    w2 = 2 * feats - w1
    units = 2 * nx
    unit = 2 * G * msg // units
    dma = lambda n: pltpu.SemaphoreType.DMA((n,))
    vm = lambda shape, dtype=BF: pltpu.VMEM(shape, dtype)
    scratch = [
        vm((2 * nz, msg, hidden)), vm((2 * nz, msg, hidden)), vm((feats, hidden)), vm((feats, hidden)), dma(5),
        vm((8, toks), F32), vm((2, feats, toks)), vm((2, feats, toks)), vm((2, 8, toks), F32),
        vm((4 * toks, w1)), vm((2 * toks, w2)),
        vm((nz, msg, w1)), vm((nz, msg, w2)), vm((2 * nz, msg, w1)), vm((2 * nz, msg, w2)),
        vm((w1, hidden)), vm((2 * nz, msg, hidden)),
        vm((C, units, unit, hidden), F32), vm((C, units, unit, hidden)), vm((C, units - 1, unit, hidden)),
        vm((C, unit, hidden), F32), vm((C, unit, hidden)), vm((C, unit, hidden)),
        vm((C, units, unit, hidden)),
        vm((2 * feats, 2 * nz * msg)), vm((2 * hidden, feats)), vm((feats, 2 * toks), F32),
        vm((2 * nz, msg, hidden)), vm((2 * nz, msg, hidden)),
        vm((2, nz, msg, feats)), vm((nz, msg, feats)), vm((nz, msg, feats)), vm((nz, msg, feats)),
        vm((2, feats, toks)), vm((2, feats, toks)),
        dma(8), dma(8), dma(nz), dma(nz), dma(nz), dma(nz), dma(nz), dma(nz), dma(nz), dma(nz),
        dma(C * (units - 1)), dma(C * (units - 1)), dma(C), dma(C), dma(C * (units - 1)), dma(C * (units - 1)),
        dma(C), dma(C), dma(nz), dma(nz), dma(2), dma(2),
    ]
    o_tok, o_gate, o_up, o_down = pl.pallas_call(
        functools.partial(kernel, (nz, nx, nzh, cap, C)),
        out_shape=(
            jax.ShapeDtypeStruct((feats, toks), BF),
            jax.ShapeDtypeStruct((feats, hidden), BF),
            jax.ShapeDtypeStruct((feats, hidden), BF),
            jax.ShapeDtypeStruct((feats, hidden), BF),
        ),
        in_specs=[pl.BlockSpec(memory_space=pltpu.VMEM)] * 4 + [pl.BlockSpec(memory_space=pltpu.HBM)] * 5,
        out_specs=(pl.BlockSpec(memory_space=pltpu.VMEM),) * 4,
        scratch_shapes=scratch,
        compiler_params=pltpu.CompilerParams(
            collective_id=0, has_side_effects=True, vmem_limit_bytes=60 * 1024 * 1024
        ),
    )(
        tokens_in.T, grad_out.T, routes.T, gate_probs.T,
        saved_gate.reshape(2 * nz, msg, hidden), saved_up.reshape(2 * nz, msg, hidden),
        w_gate[0], w_up[0], w_down[0].T,
    )
    return o_tok.T, o_gate[None], o_up[None], o_down.T[None]


def build(mesh, dp_shape, chunks):
    return jax.shard_map(
        functools.partial(shards, dp_shape, chunks),
        mesh=mesh,
        in_specs=(
            P("expert", "dp"),
            P("expert", "dp"),
            P("expert", None),
            P("expert", None),
            P("expert", None, None),
            P("expert", None, None),
            P("expert", "dp", None),
            P("expert", "dp", None),
            P("expert", None, "dp"),
        ),
        out_specs=(
            P("expert", "dp"),
            P("expert", "dp", None),
            P("expert", "dp", None),
            P("expert", None, "dp"),
        ),
        check_vma=False,
    )


def solution(mesh):
    return build(mesh, (4, 2), CHUNKS)
```

time: 181 us -> 173 us (0.956)
  the two profiles are of different devices: /device:TPU:192 before, /device:TPU:32 now
where the time goes in v2:
time: 173 us
  Pallas kernels  167 us (97%)
  local copies, waits for them, and re-layouts  5.37 us (3%)
    pallas_call x1, Pallas kernels, shards(): pl.pallas_call(functools.partial(kernel, (nz, nx, nzh, cap, C)), out_shap...  167 us
    unnamed x8, local copies, waits for them, and re-layouts  5.37 us

profile of v2, /device:TPU:32, one launch (start us, length us, event | category | flops | bytes accessed | tf_op | source)
XLA Modules:
  0.0 172.8 jit_solution(5301637582497467878)
XLA Ops:
  0.6 166.7 %shard_map.120 = (bf16[448,128]{1,0:T(8,128)(2,1)}, bf16[448,512]{1,0:T(8,128)(2,1)}, bf16[448,512]{1,0:T(8,128)(2,1)}, bf16[448,512]{1,0:T(8,128)(2,1)}) custom-call(bf16[448,128]{1,0:T(8,128)(2,1)} %bitcast.26, bf16[448,128]{1,0:T(8,128)(2,1)} %bitcast.27, s32[2,128]{1,0:T(2,128)} %bitcast.28, f32[2,128]{1,0:T(2,128)} %bitcast.29, ...), custom_call_target="tpu_custom_call" | custom-call | tf_op jit(solution)/shard_map/pallas_call | solution.py:445
  167.4 1.6 copy.17
  168.9 0.0 copy-start.1
  168.9 1.9 %copy.18 = bf16[1,448,512]{2,1,0:T(8,128)(2,1)} copy(bf16[1,448,512]{2,1,0:T(8,128)(2,1)} %bitcast.21) | data formatting | bytes 917504
  170.8 0.0 copy-done.1
  170.8 0.0 copy-start
  170.8 0.8 copy.19
  171.6 0.4 copy-done
  172.0 0.8 copy.20
Async XLA Ops:
  168.9 1.9 %copy-start.1 = (bf16[448,512]{1,0:T(8,128)(2,1)S(1)}, bf16[448,512]{1,0:T(8,128)(2,1)}, u32[]{:S(2)}) copy-start(bf16[448,512]{1,0:T(8,128)(2,1)} %get-tuple-element.10) | copy-start | bytes 1376260
  170.8 1.2 copy-start

commit v3 on v2

--- a/solution.py
+++ b/solution.py
@@ -34,10 +34,10 @@
     meta, r_tok, r_grad, r_meta, pack_b, pack_c,
     sb1, sb2, x1, x2, wd, act,
     p32, pb, rx, w32, wb, rz, hid,
-    xt, wt, out32, gg, ug, bg, rp, ps, rr, ot, ro,
+    xt, wt, out32, gg, ug, bg, rp, ps, pt, rr, rt, ot, ro,
     sem_ys, sem_yr, sem_z1s, sem_z1r, sem_f1s, sem_f1r, sem_z2s, sem_z2r, sem_f2s, sem_f2r,
     sem_xs, sem_xr, sem_hs, sem_hr, sem_gs, sem_gr,
-    sem_ps, sem_pr, sem_rs, sem_rr, sem_os, sem_or,
+    sem_ps, sem_pr, sem_rs, sem_rr, sem_ts, sem_tr, sem_os, sem_or,
 ):
     nz, nx, nzh, cap, C = cfg
     G = nz // C
@@ -47,6 +47,7 @@
     msg = 2 * cap
     units = 2 * nx
     rows = 2 * G * msg
+    wide, half = ps.shape[2], pt.shape[1]
 
     e = lax.axis_index("expert")
     d = lax.axis_index("dp")
@@ -263,6 +264,10 @@
     def r_copy(c, j):
         to = recv_z(c, j)
         return remote(ps.at[to], rr.at[z], sem_rs.at[c * G + j], sem_rr.at[c * G + j], to * Y + y, d)
+
+    def t_copy(c, j):
+        to = recv_z(c, j)
+        return remote(pt.at[to], rt.at[z], sem_ts.at[c * G + j], sem_tr.at[c * G + j], to * Y + y, d)
 
     def stage_forward(c):
         def body(j):
@@ -319,16 +324,26 @@
     def stage_pair(c):
         p_copy(c).wait_recv()
         at = pl.ds(group(c) * G, G)
-        ps[at] = (bg[h, at].astype(F32) + rp[at].astype(F32)).astype(BF)
+        total = (bg[h, at].astype(F32) + rp[at].astype(F32)).astype(BF)
+        ps[at] = total[:, :, 0:wide]
+        tail = total[:, :, wide:]
+        below = jnp.concatenate([tail[:, half:], jnp.zeros((G, 2 * half - msg, feats - wide), BF)], axis=1)
+        pt[at] = jnp.concatenate([tail[:, 0:half], below], axis=2)
         if c == 0:
             rr[z] = ps[z]
-        loop(first(c), G, lambda j: r_copy(c, j).start())
-
-    def stage_second(c):
-        send_second(c)
-
-    stages = [stage_forward, stage_product, stage_sum, stage_second, stage_zh, stage_hidden, stage_pair]
-    fillers = {0: fill_second, 1: fill_weights, 2: fill_activation, C + 1: fill_down}
+            rt[z] = pt[z]
+        loop(first(c), G, lambda j: (r_copy(c, j).start(), t_copy(c, j).start()))
+
+    def stage_gap(c):
+        pass
+
+    def fill_both():
+        for c in reversed(range(C)):
+            send_second(c)
+        fill_down()
+
+    stages = [stage_forward, stage_product, stage_sum, stage_gap, stage_zh, stage_hidden, stage_pair]
+    fillers = {0: fill_second, 1: fill_weights, 2: fill_activation, C + 1: fill_both}
     for step in range(C + len(stages) - 1):
         for s in reversed(range(len(stages))):
             c = step - s
@@ -351,11 +366,20 @@
         out[...] = dot_nn(xt[feats : 2 * feats, :], grads[...].reshape(total_rows, hidden)).astype(BF)
 
     for c in range(C):
-        loop(first(c), G, lambda j: r_copy(c, j).wait_recv())
+        loop(first(c), G, lambda j: (r_copy(c, j).wait_recv(), t_copy(c, j).wait_recv()))
         g, one_hot = picks(c)
-        back_rows = rr[pl.ds(g * G, G)].reshape(G * msg, feats)
-        part = dot_tn(back_rows, one_hot)
-        out32[...] = part if c == 0 else out32[...] + part
+        part = dot_tn(rr[pl.ds(g * G, G)].reshape(G * msg, wide), one_hot)
+        split = one_hot.reshape(G, msg, 2 * toks)
+        tails = rt[pl.ds(g * G, G)].reshape(G * half, 128)
+        above = split[:, 0:half].reshape(G * half, 2 * toks)
+        below = jnp.concatenate([split[:, half:], jnp.zeros((G, 2 * half - msg, 2 * toks), BF)], axis=1)
+        left = dot_tn(tails, above)[0:64] + dot_tn(tails, below.reshape(G * half, 2 * toks))[64:]
+        if c == 0:
+            out32[0:wide] = part
+            out32[wide:] = left
+        else:
+            out32[0:wide] += part
+            out32[wide:] += left
 
     def o_copy(i, j):
         return remote(ot.at[i], ro.at[par], sem_os.at[i], sem_or.at[j], z * Y + 2 * h + i, d)
@@ -391,6 +415,7 @@
             z1_copy(c, j).wait_send()
             z2_copy(c, j).wait_send()
             r_copy(c, j).wait_send()
+            t_copy(c, j).wait_send()
 
         loop(first(c), G, sent)
 
@@ -421,6 +446,7 @@
     G = nz // C
     w1 = -(-feats // 128) * 128
     w2 = 2 * feats - w1
+    wide, half = feats - 64, -(-msg // 16) * 8
     units = 2 * nx
     unit = 2 * G * msg // units
     dma = lambda n: pltpu.SemaphoreType.DMA((n,))
@@ -436,11 +462,12 @@
         vm((C, units, unit, hidden)),
         vm((2 * feats, 2 * nz * msg)), vm((2 * hidden, feats)), vm((feats, 2 * toks), F32),
         vm((2 * nz, msg, hidden)), vm((2 * nz, msg, hidden)),
-        vm((2, nz, msg, feats)), vm((nz, msg, feats)), vm((nz, msg, feats)), vm((nz, msg, feats)),
+        vm((2, nz, msg, feats)), vm((nz, msg, feats)),
+        vm((nz, msg, wide)), vm((nz, half, 128)), vm((nz, msg, wide)), vm((nz, half, 128)),
         vm((2, feats, toks)), vm((2, feats, toks)),
         dma(8), dma(8), dma(nz), dma(nz), dma(nz), dma(nz), dma(nz), dma(nz), dma(nz), dma(nz),
         dma(C * (units - 1)), dma(C * (units - 1)), dma(C), dma(C), dma(C * (units - 1)), dma(C * (units - 1)),
-        dma(C), dma(C), dma(nz), dma(nz), dma(2), dma(2),
+        dma(C), dma(C), dma(nz), dma(nz), dma(nz), dma(nz), dma(2), dma(2),
     ]
     o_tok, o_gate, o_up, o_down = pl.pallas_call(
         functools.partial(kernel, (nz, nx, nzh, cap, C)),

time: 173 us -> 168 us (0.971)
  Pallas kernels: 167 us -> 162 us
    pallas_call x1, Pallas kernels: 167 us -> 162 us  [shards(): pl.pallas_call(functools.partial(kernel, (nz, nx, nzh, cap, C)), out_shap...]
where the time goes in v3:
time: 168 us
  Pallas kernels  162 us (96%)
  local copies, waits for them, and re-layouts  5.37 us (3%)
    pallas_call x1, Pallas kernels, shards(): pl.pallas_call(functools.partial(kernel, (nz, nx, nzh, cap, C)), out_shap...  162 us
    unnamed x8, local copies, waits for them, and re-layouts  5.37 us

profile of v3, /device:TPU:32, one launch (start us, length us, event | category | flops | bytes accessed | tf_op | source)
XLA Modules:
  0.0 167.9 jit_solution(3227462364587743573)
XLA Ops:
  0.6 161.9 %shard_map.120 = (bf16[448,128]{1,0:T(8,128)(2,1)}, bf16[448,512]{1,0:T(8,128)(2,1)}, bf16[448,512]{1,0:T(8,128)(2,1)}, bf16[448,512]{1,0:T(8,128)(2,1)}) custom-call(bf16[448,128]{1,0:T(8,128)(2,1)} %bitcast.26, bf16[448,128]{1,0:T(8,128)(2,1)} %bitcast.27, s32[2,128]{1,0:T(2,128)} %bitcast.28, f32[2,128]{1,0:T(2,128)} %bitcast.29, ...), custom_call_target="tpu_custom_call" | custom-call | tf_op jit(solution)/shard_map/pallas_call | solution.py:472
  162.5 1.6 copy.17
  164.1 0.0 copy-start.1
  164.1 1.9 %copy.18 = bf16[1,448,512]{2,1,0:T(8,128)(2,1)} copy(bf16[1,448,512]{2,1,0:T(8,128)(2,1)} %bitcast.21) | data formatting | bytes 917504
  166.0 0.0 copy-done.1
  166.0 0.0 copy-start
  166.0 0.8 copy.19
  166.7 0.4 copy-done
  167.1 0.8 copy.20
Async XLA Ops:
  164.1 1.9 %copy-start.1 = (bf16[448,512]{1,0:T(8,128)(2,1)S(1)}, bf16[448,512]{1,0:T(8,128)(2,1)}, u32[]{:S(2)}) copy-start(bf16[448,512]{1,0:T(8,128)(2,1)} %get-tuple-element.10) | copy-start | bytes 1376260
  166.0 1.2 copy-start

commit v4 on v3

--- a/solution.py
+++ b/solution.py
@@ -360,12 +360,6 @@
         loop(first(c), G, forward2)
 
     for c in range(C):
-        loop(0, G, lambda j: f2_copy(c, j).wait_recv())
-    turn(x2, w1)
-    for grads, out in ((gg, o_gate), (ug, o_up)):
-        out[...] = dot_nn(xt[feats : 2 * feats, :], grads[...].reshape(total_rows, hidden)).astype(BF)
-
-    for c in range(C):
         loop(first(c), G, lambda j: (r_copy(c, j).wait_recv(), t_copy(c, j).wait_recv()))
         g, one_hot = picks(c)
         part = dot_tn(rr[pl.ds(g * G, G)].reshape(G * msg, wide), one_hot)
@@ -396,6 +390,12 @@
         @pl.when(s == y)
         def _():
             ro[par] = ot[i]
+
+    for c in range(C):
+        loop(0, G, lambda j: f2_copy(c, j).wait_recv())
+    turn(x2, w1)
+    for grads, out in ((gg, o_gate), (ug, o_up)):
+        out[...] = dot_nn(xt[feats : 2 * feats, :], grads[...].reshape(total_rows, hidden)).astype(BF)
 
     for j in range(2):
         @pl.when(y // 2 + 2 * j != y)

time: 168 us -> 168 us (level)
  no operation moved by 1% of the time
where the time goes in v4:
time: 168 us
  Pallas kernels  162 us (96%)
  local copies, waits for them, and re-layouts  5.37 us (3%)
    pallas_call x1, Pallas kernels, shards(): pl.pallas_call(functools.partial(kernel, (nz, nx, nzh, cap, C)), out_shap...  162 us
    unnamed x8, local copies, waits for them, and re-layouts  5.37 us

profile of v4, /device:TPU:32, one launch (start us, length us, event | category | flops | bytes accessed | tf_op | source)
XLA Modules:
  0.0 167.9 jit_solution(17880055347748320992)
XLA Ops:
  0.6 161.9 %shard_map.120 = (bf16[448,128]{1,0:T(8,128)(2,1)}, bf16[448,512]{1,0:T(8,128)(2,1)}, bf16[448,512]{1,0:T(8,128)(2,1)}, bf16[448,512]{1,0:T(8,128)(2,1)}) custom-call(bf16[448,128]{1,0:T(8,128)(2,1)} %bitcast.26, bf16[448,128]{1,0:T(8,128)(2,1)} %bitcast.27, s32[2,128]{1,0:T(2,128)} %bitcast.28, f32[2,128]{1,0:T(2,128)} %bitcast.29, ...), custom_call_target="tpu_custom_call" | custom-call | tf_op jit(solution)/shard_map/pallas_call | solution.py:472
  162.5 1.6 copy.17
  164.1 0.0 copy-start.1
  164.1 1.9 %copy.18 = bf16[1,448,512]{2,1,0:T(8,128)(2,1)} copy(bf16[1,448,512]{2,1,0:T(8,128)(2,1)} %bitcast.21) | data formatting | bytes 917504
  166.0 0.0 copy-done.1
  166.0 0.0 copy-start
  166.0 0.8 copy.19
  166.7 0.4 copy-done
  167.1 0.8 copy.20
Async XLA Ops:
  164.1 1.9 %copy-start.1 = (bf16[448,512]{1,0:T(8,128)(2,1)S(1)}, bf16[448,512]{1,0:T(8,128)(2,1)}, u32[]{:S(2)}) copy-start(bf16[448,512]{1,0:T(8,128)(2,1)} %get-tuple-element.10) | copy-start | bytes 1376260
  166.0 1.2 copy-start
